TPU v7x, 256 devices: a whole 4x4x8 slice. The times are simulated.
256 devices in a mesh: enc: 16 (over x, y), blk: 16 (over z, core).
Axes of the slice: x: 4, y: 4, z: 8, core: 2. Of those that a mesh axis runs over, the one named last changes fastest.
Arguments:
- observations: bfloat16 [131072, 128], P(('enc', 'blk')), may hold values from -6 to 6
- lon_index: int32 [256, 512], P(('enc', 'blk')), may hold values from 0 to 1439
- live_count: int32 [256, 256], P(('enc', 'blk')), may hold values from 0 to 2, as said below
- w_in: bfloat16 [128, 512], replicated, may hold values from -0.5 to 0.5
- w_out: bfloat16 [512, 512], replicated, may hold values from -0.25 to 0.25
- w_spec: float32 [256, 512], replicated, may hold values from -4 to 4
- north: float32 [256, 512], P(('enc', 'blk')), may hold values from -0.8 to 0.8
- south: float32 [256, 512], P(('enc', 'blk')), may hold values from -0.8 to 0.8
- w_mix: bfloat16 [512, 512], replicated, may hold values from -0.25 to 0.25
- loss_sensitivity: bfloat16 [256, 1440, 512], P(('enc', 'blk')), may hold values from -6 to 6
Outputs:
- predicted_state: bfloat16 [256, 1440, 512], P(('enc', 'blk'))
- entry_matrix_slope: float32 [128, 512], replicated
- exit_matrix_slope: float32 [512, 512], replicated
- blend_matrix_slope: float32 [512, 512], replicated
- observation_slope: bfloat16 [131072, 128], P(('enc', 'blk'))
Inputs may be any that keep to these rules, and one draw needn't show every extreme that they name: In every draw some cycle r has live_count[r, s] = 2 for every source s.
All inputs are finite; a program needn't handle non-finite values.
Results may differ from a plain program's by a relative error of at most 0.0095.
Values may be sent and summed in bfloat16 or wider, within the bound.
No kernel may reach another device: no remote copies, remote signals or barrier semaphores. Data moves between devices by JAX's collectives and lax.ppermute only.
A program may use at most 64 MiB of HBM per device.

v0:
```python
import math
import jax
import jax.numpy as jnp
from jax import lax
from jax.sharding import PartitionSpec as P

CODE_BREADTH = 512
LON = 1440
MODES = 128
CAP = 2


def extended(block, sides, width):
    for axis, dim in sides:
        count = lax.axis_size(axis)
        forward = [(i, i + 1) for i in range(count - 1)]
        backward = [(target, source) for source, target in forward]
        low = lax.ppermute(
            lax.slice_in_dim(block, block.shape[dim] - width, None, axis=dim), axis, forward
        )
        high = lax.ppermute(lax.slice_in_dim(block, 0, width, axis=dim), axis, backward)
        block = jnp.concatenate([low, block, high], axis=dim)
    return block


def from_behind(value, axis, steps):
    count = lax.axis_size(axis)
    initial, last = (max(0, -steps), min(count, count - steps))
    return lax.ppermute(value, axis, [(source, source + steps) for source in range(initial, last)])


def tables():
    wavenum = jnp.arange(MODES, dtype=jnp.int32)
    lon_pos = jnp.arange(LON, dtype=jnp.int32)
    phases = (wavenum[:, None] * lon_pos[None, :] % LON).astype(jnp.float32) * (2.0 * math.pi / LON)
    forward = jnp.concatenate([jnp.cos(phases), -jnp.sin(phases)], 0).astype(jnp.bfloat16)
    weight = jnp.where(wavenum == 0, 1.0, 2.0).astype(jnp.float32) / LON
    inverse = jnp.concatenate(
        [jnp.cos(phases) * weight[:, None], -jnp.sin(phases) * weight[:, None]], 0
    ).T.astype(jnp.bfloat16)
    return (forward, inverse)


def silu_grad(values):
    logistic = jax.nn.sigmoid(values)
    return logistic * (1.0 + values * (1.0 - logistic))


def cell_table(lon_row, count_row):
    is_live = (jnp.arange(CAP, dtype=jnp.int32)[None, :] < count_row[:, None]).reshape(-1)
    matches = (lon_row[None, :] == jnp.arange(LON, dtype=jnp.int32)[:, None]) & is_live[None, :]
    return (matches.astype(jnp.bfloat16), jnp.sum(matches.astype(jnp.float32), axis=1))


def encode(rows, w_in, w_out):
    pre1 = jnp.dot(rows, w_in, preferred_element_type=jnp.float32)
    hidden = jax.nn.silu(pre1).astype(jnp.bfloat16)
    latent = jnp.dot(hidden, w_out, preferred_element_type=jnp.float32).astype(jnp.bfloat16)
    return (pre1, hidden, latent)


def encoder_grads(rows, pre1, hidden, grad_latent, w_in, w_out):
    out_local = jnp.dot(hidden.T, grad_latent, preferred_element_type=jnp.float32)
    grad_hidden = jnp.dot(grad_latent, w_out.T, preferred_element_type=jnp.float32)
    grad_pre1 = (grad_hidden * silu_grad(pre1)).astype(jnp.bfloat16)
    in_local = jnp.dot(rows.T, grad_pre1, preferred_element_type=jnp.float32)
    row_grads = jnp.dot(grad_pre1, w_in.T, preferred_element_type=jnp.float32).astype(jnp.bfloat16)
    return (in_local, out_local, row_grads)


def shards(
    observations, lon_index, live_count, w_in, w_out, w_spec, north, south, w_mix, loss_sensitivity
):
    enc_count = lax.axis_size("enc")
    blk_count = lax.axis_size("blk")
    devices = enc_count * blk_count
    slot_total = observations.shape[0]
    forward, inverse = tables()
    pre1, hidden, latent = encode(observations, w_in, w_out)
    outgoing = latent.reshape(enc_count, blk_count, CAP, CODE_BREADTH)
    arrived = lax.all_to_all(
        lax.all_to_all(outgoing, "enc", split_axis=0, concat_axis=0, tiled=True),
        "blk",
        split_axis=1,
        concat_axis=1,
        tiled=True,
    )
    lat_rows = arrived.reshape(slot_total, CODE_BREADTH)
    onehot, occupancy = cell_table(lon_index[0], live_count[0])
    denom = jnp.maximum(occupancy, 1.0)[:, None]
    grid_sum = jnp.dot(onehot, lat_rows, preferred_element_type=jnp.float32)
    resampled_field = (grid_sum / denom).astype(jnp.bfloat16)
    spectrum = jnp.dot(forward, resampled_field, preferred_element_type=jnp.float32)
    border = extended(resampled_field[None], ((("enc", "blk"), 0),), 1)
    spec_prev = jnp.dot(forward, border[0], preferred_element_type=jnp.float32)
    spec_next = jnp.dot(forward, border[2], preferred_element_type=jnp.float32)
    north_row = north[0][None, :]
    south_row = south[0][None, :]
    blended_fourier_modes = (
        spectrum * w_spec + north_row * spec_prev + south_row * spec_next
    ).astype(jnp.bfloat16)
    azimuth = jnp.dot(inverse, blended_fourier_modes, preferred_element_type=jnp.float32).astype(
        jnp.bfloat16
    )
    before_nonlinearity = jnp.dot(azimuth, w_mix, preferred_element_type=jnp.float32)
    predicted_state = (
        resampled_field.astype(jnp.float32) + jax.nn.silu(before_nonlinearity)
    ).astype(jnp.bfloat16)
    grad_pre = (loss_sensitivity[0].astype(jnp.float32) * silu_grad(before_nonlinearity)).astype(
        jnp.bfloat16
    )
    mix_local = jnp.dot(azimuth.T, grad_pre, preferred_element_type=jnp.float32)
    gridding_factor = 1.0 / math.sqrt(devices * LON)
    grad_az = jnp.dot(grad_pre, w_mix.T, preferred_element_type=jnp.float32).astype(jnp.bfloat16)
    blend_matrix_slope_local = jnp.dot(inverse.T, grad_az, preferred_element_type=jnp.float32)
    from_next = from_behind(north_row * blend_matrix_slope_local, ("enc", "blk"), -1)
    from_prev = from_behind(south_row * blend_matrix_slope_local, ("enc", "blk"), 1)
    grad_spec = (w_spec * blend_matrix_slope_local + from_next + from_prev).astype(jnp.bfloat16)
    grad_grid = loss_sensitivity[0].astype(jnp.float32) + jnp.dot(
        forward.T, grad_spec, preferred_element_type=jnp.float32
    )
    scaled = (grad_grid / denom).astype(jnp.bfloat16)
    grad_rows = jnp.dot(onehot.T, scaled, preferred_element_type=jnp.float32).astype(jnp.bfloat16)
    returned = lax.all_to_all(
        lax.all_to_all(
            grad_rows.reshape(enc_count, blk_count, CAP, CODE_BREADTH),
            "enc",
            split_axis=0,
            concat_axis=0,
            tiled=True,
        ),
        "blk",
        split_axis=1,
        concat_axis=1,
        tiled=True,
    )
    grad_latent = returned.reshape(slot_total, CODE_BREADTH)
    in_local, out_local, observation_slope = encoder_grads(
        observations, pre1, hidden, grad_latent, w_in, w_out
    )
    observed_factor = 1.0 / math.sqrt(devices * slot_total)
    input_gradient_total, output_gradient_total, blend_matrix_slope_summed = lax.psum(
        (in_local, out_local, mix_local), ("enc", "blk")
    )
    return (
        predicted_state[None],
        input_gradient_total * observed_factor,
        output_gradient_total * observed_factor,
        blend_matrix_slope_summed * gridding_factor,
        observation_slope,
    )


def solution(mesh):
    placed = (
        P(("enc", "blk"), None),
        P(("enc", "blk"), None),
        P(("enc", "blk"), None),
        P(),
        P(),
        P(),
        P(("enc", "blk"), None),
        P(("enc", "blk"), None),
        P(),
        P(("enc", "blk"), None, None),
    )
    return jax.shard_map(
        shards,
        mesh=mesh,
        in_specs=placed,
        out_specs=(P(("enc", "blk"), None, None), P(), P(), P(), P(("enc", "blk"), None)),
        check_vma=False,
    )
```

profile of v0, /device:TPU:8, one launch (start us, length us, event | category | flops | bytes accessed | tf_op | source)
XLA Modules:
  0.0 426.9 jit_solution(8997733929521939271)
XLA Ops:
  9.5 1.5 convolution_convert_fusion.2
  11.2 17.3 %all_to_all.20 = bf16[16,16,2,512]{3,2,1,0:T(2,128)(2,1)S(1)} all-to-all(bf16[16,16,2,512]{3,2,1,0:T(2,128)(2,1)S(1)} %reshape.48), channel_id=1, replica_groups=mesh['enc'=16,'blk'=16] {'enc'}, dimensions={0} | all-to-all | bytes 1048576 | tf_op jit(solution)/shard_map/all_to_all | solution.py:82
  29.8 8.6 %all-to-all-start.1 = ((bf16[16,16,2,512]{3,2,0,1:T(2,128)(2,1)}), bf16[16,16,2,512]{3,2,0,1:T(2,128)(2,1)S(1)}, u32[]{:S(2)}, u32[]{:S(2)}) async-start(bf16[16,16,2,512]{3,2,0,1:T(2,128)(2,1)} %copy.30), calls=%async_computation.1 | async-start | bytes 1048576 | tf_op jit(solution)/shard_map/all_to_all | solution.py:81
  39.2 15.2 %all-to-all-done.1 = bf16[16,16,2,512]{3,2,0,1:T(2,128)(2,1)S(1)} async-done(((bf16[16,16,2,512]{3,2,0,1:T(2,128)(2,1)}), bf16[16,16,2,512]{3,2,0,1:T(2,128)(2,1)S(1)}, u32[]{:S(2)}, u32[]{:S(2)}) %all-to-all-start.1) | async-done | bytes 524320 | tf_op jit(solution)/shard_map/all_to_all | solution.py:81
  56.1 2.9 collective-permute-start.1
  59.1 2.7 collective-permute-start
  61.8 3.5 fusion.44
  65.3 4.1 multiply_convert_fusion.2
  70.8 5.2 %collective-permute-done.1 = bf16[1,1440,512]{2,1,0:T(8,128)(2,1)S(1)} collective-permute-done((bf16[1,1440,512]{2,1,0:T(8,128)(2,1)S(1)}, bf16[1,1440,512]{2,1,0:T(8,128)(2,1)S(1)}, u32[]{:S(2)}, u32[]{:S(2)}) %collective-permute-start.1) | collective-permute-done | bytes 1474592 | tf_op jit(solution)/shard_map/ppermute | solution.py:21
  77.3 4.6 %collective-permute-done = bf16[1,1440,512]{2,1,0:T(8,128)(2,1)S(1)} collective-permute-done((bf16[1,1440,512]{2,1,0:T(8,128)(2,1)S(1)}, bf16[1,1440,512]{2,1,0:T(8,128)(2,1)S(1)}, u32[]{:S(2)}, u32[]{:S(2)}) %collective-permute-start) | collective-permute-done | bytes 1474592 | tf_op jit(solution)/shard_map/ppermute | solution.py:18
  83.0 2.9 convolution_convert_fusion.1
  85.9 5.2 %fusion = (bf16[1440,512]{1,0:T(8,128)(2,1)S(1)}, bf16[1,1440,512]{2,1,0:T(8,128)(2,1)}) fusion(bf16[1,1440,512]{2,1,0:T(8,128)(2,1)} %param.19, bf16[1440,512]{1,0:T(8,128)(2,1)} %copy-done.12, bf16[1440,512]{1,0:T(8,128)(2,1)S(1)} %convolution_convert_fusion.1, bf16[512,512]{1,0:T(8,128)(2,1)S(1)} %copy-done), kind=kOutput, calls=%fused_computation.4 | convolution fusion | flops 765296640 | bytes 7897088 | tf_op jit(solution)/shard_map/dot_general | solution.py:105
  91.1 4.2 broadcast_multiply_fusion.3
  95.3 1.9 collective-permute-start.2
  97.2 2.6 collective-permute-start.3
  99.8 4.4 %collective-permute-done.2 = f32[256,512]{1,0:T(8,128)S(1)} collective-permute-done((f32[256,512]{1,0:T(8,128)}, f32[256,512]{1,0:T(8,128)S(1)}, u32[]{:S(2)}, u32[]{:S(2)}) %collective-permute-start.2) | collective-permute-done | bytes 524320 | tf_op jit(solution)/shard_map/ppermute | solution.py:29
  104.2 5.8 %collective-permute-done.3 = f32[256,512]{1,0:T(8,128)S(1)} collective-permute-done((f32[256,512]{1,0:T(8,128)}, f32[256,512]{1,0:T(8,128)S(1)}, u32[]{:S(2)}, u32[]{:S(2)}) %collective-permute-start.3) | collective-permute-done | bytes 524320 | tf_op jit(solution)/shard_map/ppermute | solution.py:29
  110.8 3.9 fusion.17
  115.0 16.4 %all_to_all.21 = bf16[16,16,2,512]{3,2,1,0:T(2,128)(2,1)S(1)} all-to-all(bf16[16,16,2,512]{3,2,1,0:T(2,128)(2,1)S(1)} %reshape.50), channel_id=1, replica_groups=mesh['enc'=16,'blk'=16] {'enc'}, dimensions={0} | all-to-all | bytes 1048576 | tf_op jit(solution)/shard_map/all_to_all | solution.py:125
  132.6 3.6 all-to-all-start.3
  136.2 3.3 fusion.53
  139.6 12.5 %all-to-all-done.3 = bf16[16,16,2,512]{3,2,0,1:T(2,128)(2,1)S(1)} async-done(((bf16[16,16,2,512]{3,2,0,1:T(2,128)(2,1)}), bf16[16,16,2,512]{3,2,0,1:T(2,128)(2,1)S(1)}, u32[]{:S(2)}, u32[]{:S(2)}) %all-to-all-start.3) | async-done | bytes 524320 | tf_op jit(solution)/shard_map/all_to_all | solution.py:124
  152.8 2.0 fusion.20
  158.3 257.6 %all-reduce.3.cloned.1.call-done = (f32[128,512]{0,1:T(8,128)}, f32[512,512]{1,0:T(8,128)}, f32[512,512]{1,0:T(8,128)}) async-done(((f32[128,512]{0,1:T(8,128)}, f32[512,512]{1,0:T(8,128)}, f32[512,512]{1,0:T(8,128)}), (f32[128,512]{0,1:T(8,128)}, f32[512,512]{1,0:T(8,128)}, f32[512,512]{1,0:T(8,128)})) %all-reduce.3.cloned.1.call-update) | async-done | bytes 2359312 | tf_op jit(solution)/shard_map/psum | solution.py:142
  (66 shorter events, 20.9 us)
Async XLA Ops:
  7.2 78.7 %copy-start = (bf16[512,512]{1,0:T(8,128)(2,1)S(1)}, bf16[512,512]{1,0:T(8,128)(2,1)}, u32[]{:S(2)}) copy-start(bf16[512,512]{1,0:T(8,128)(2,1)} %param.18) | copy-start | bytes 1572868
  11.2 27.2 %copy-start.11 = (s32[1,256]{1,0:T(1,128)S(1)}, s32[1,256]{1,0:T(1,128)}, u32[]{:S(2)}) copy-start(s32[1,256]{1,0:T(1,128)} %param.12) | copy-start | bytes 3076
  11.2 27.5 %copy-start.19 = (s32[1,512]{1,0:T(1,128)S(1)}, s32[1,512]{1,0:T(1,128)}, u32[]{:S(2)}) copy-start(s32[1,512]{1,0:T(1,128)} %param.11) | copy-start | bytes 6148
  29.8 24.6 %all-to-all-start.1 = ((bf16[16,16,2,512]{3,2,0,1:T(2,128)(2,1)}), bf16[16,16,2,512]{3,2,0,1:T(2,128)(2,1)S(1)}, u32[]{:S(2)}, u32[]{:S(2)}) async-start(bf16[16,16,2,512]{3,2,0,1:T(2,128)(2,1)} %copy.30), calls=%async_computation.1 | async-start | bytes 1048576 | tf_op jit(solution)/shard_map/all_to_all | solution.py:81
  56.1 14.7 %copy-start.12 = (bf16[1440,512]{1,0:T(8,128)(2,1)}, bf16[1440,512]{1,0:T(8,128)(2,1)S(1)}, u32[]{:S(2)}) copy-start(bf16[1440,512]{1,0:T(8,128)(2,1)S(1)} %divide_convert_fusion.1) | copy-start | bytes 4423684
  56.1 13.3 %copy-start.14 = (f32[256,512]{1,0:T(8,128)S(1)}, f32[256,512]{1,0:T(8,128)}, u32[]{:S(2)}) copy-start(f32[256,512]{1,0:T(8,128)} %param.15) | copy-start | bytes 1572868
  56.1 19.8 %collective-permute-start.1 = (bf16[1,1440,512]{2,1,0:T(8,128)(2,1)S(1)}, bf16[1,1440,512]{2,1,0:T(8,128)(2,1)S(1)}, u32[]{:S(2)}, u32[]{:S(2)}) collective-permute-start(bf16[1,1440,512]{2,1,0:T(8,128)(2,1)S(1)} %bitcast.52), channel_id=1, source_target_pairs={{1,0},{2,1},{3,2},{4,3},{5,4},{6,5},{7,6},{8,7},{9,8},{10,9},{11,1... | collective-permute-start | bytes 4423688 | tf_op jit(solution)/shard_map/ppermute | solution.py:21
  59.1 22.8 %collective-permute-start = (bf16[1,1440,512]{2,1,0:T(8,128)(2,1)S(1)}, bf16[1,1440,512]{2,1,0:T(8,128)(2,1)S(1)}, u32[]{:S(2)}, u32[]{:S(2)}) collective-permute-start(bf16[1,1440,512]{2,1,0:T(8,128)(2,1)S(1)} %bitcast.53), channel_id=1, source_target_pairs={{0,1},{1,2},{2,3},{3,4},{4,5},{5,6},{6,7},{7,8},{8,9},{9,10},{10,1... | collective-permute-start | bytes 4423688 | tf_op jit(solution)/shard_map/ppermute | solution.py:18
  65.3 17.7 %copy-start.8 = (bf16[128,1440]{1,0:T(8,128)(2,1)}, bf16[128,1440]{1,0:T(8,128)(2,1)S(1)}, u32[]{:S(2)}) copy-start(bf16[128,1440]{1,0:T(8,128)(2,1)S(1)} %get-tuple-element.45) | copy-start | bytes 1105924
  65.3 17.7 %copy-start.9 = (bf16[128,1440]{1,0:T(8,128)(2,1)}, bf16[128,1440]{1,0:T(8,128)(2,1)S(1)}, u32[]{:S(2)}) copy-start(bf16[128,1440]{1,0:T(8,128)(2,1)S(1)} %get-tuple-element.46) | copy-start | bytes 1105924
  69.4 13.6 %copy-start.10 = (bf16[128,1440]{1,0:T(8,128)(2,1)}, bf16[128,1440]{1,0:T(8,128)(2,1)S(1)}, u32[]{:S(2)}) copy-start(bf16[128,1440]{1,0:T(8,128)(2,1)S(1)} %get-tuple-element.42) | copy-start | bytes 1105924
  69.4 6.5 %copy-start.17 = (f32[1,512]{1,0:T(1,128)S(1)}, f32[1,512]{1,0:T(1,128)}, u32[]{:S(2)}) copy-start(f32[1,512]{1,0:T(1,128)} %param.17) | copy-start | bytes 6148
  76.0 7.1 %copy-start.18 = (f32[1,512]{1,0:T(1,128)S(1)}, f32[1,512]{1,0:T(1,128)}, u32[]{:S(2)}) copy-start(f32[1,512]{1,0:T(1,128)} %param.16) | copy-start | bytes 6148
  81.9 1.1 copy-start.13
  91.1 4.2 copy-start.1
  95.3 8.9 %collective-permute-start.2 = (f32[256,512]{1,0:T(8,128)}, f32[256,512]{1,0:T(8,128)S(1)}, u32[]{:S(2)}, u32[]{:S(2)}) collective-permute-start(f32[256,512]{1,0:T(8,128)} %get-tuple-element.40), channel_id=1, source_target_pairs={{1,0},{2,1},{3,2},{4,3},{5,4},{6,5},{7,6},{8,7},{9,8},{10,9},{11,1... | collective-permute-start | bytes 1572872 | tf_op jit(solution)/shard_map/ppermute | solution.py:29
  97.2 12.8 %collective-permute-start.3 = (f32[256,512]{1,0:T(8,128)}, f32[256,512]{1,0:T(8,128)S(1)}, u32[]{:S(2)}, u32[]{:S(2)}) collective-permute-start(f32[256,512]{1,0:T(8,128)} %get-tuple-element.41), channel_id=1, source_target_pairs={{0,1},{1,2},{2,3},{3,4},{4,5},{5,6},{6,7},{7,8},{8,9},{9,10},{10,1... | collective-permute-start | bytes 1572872 | tf_op jit(solution)/shard_map/ppermute | solution.py:29
  132.6 19.5 %all-to-all-start.3 = ((bf16[16,16,2,512]{3,2,0,1:T(2,128)(2,1)}), bf16[16,16,2,512]{3,2,0,1:T(2,128)(2,1)S(1)}, u32[]{:S(2)}, u32[]{:S(2)}) async-start(bf16[16,16,2,512]{3,2,0,1:T(2,128)(2,1)} %copy.32), calls=%async_computation.3 | async-start | bytes 1048576 | tf_op jit(solution)/shard_map/all_to_all | solution.py:124
  136.2 279.7 %all-reduce.3.cloned.1.call-start = ((), (), s32[]{:S(2)}) async-start(), calls=%async_computation.4 | async-start | bytes 4718592 | tf_op jit(solution)/shard_map/psum | solution.py:142
  139.6 13.2 %copy-start.15 = (bf16[512,512]{1,0:T(8,128)(2,1)S(1)}, bf16[512,512]{1,0:T(8,128)(2,1)}, u32[]{:S(2)}) copy-start(bf16[512,512]{1,0:T(8,128)(2,1)} %param.14) | copy-start | bytes 1572868
  152.8 2.0 copy-start.3
  154.8 1.5 copy-start.6
  415.9 2.0 copy-start.5
  415.9 3.1 copy-start.4
  (3 other events, 2.8 us)
Sparse Core Ops, SparseCore 0:
  157.5 258.3 all-reduce.2
where the time goes:
time: 428 us; the launch traced here: 427 us
  waiting for transfers between devices  305 us (71%)
  blocking collectives  33.7 us (8%)
  matrix products  31.5 us (7%)
  starting transfers between devices  22.3 us (5%)
  between operations  14.3 us (3%)
  other arithmetic  11.5 us (3%)
  local copies, waits for them, and re-layouts  8.33 us (2%)
    psum x1, waiting for transfers between devices, shards(): lax.psum((in_local, out_local, mix_local), ('enc', 'blk'))  258 us
    all_to_all x1, blocking collectives, shards(): lax.all_to_all(outgoing, 'enc', split_axis=0, concat_axis=0, tiled=True)  17.3 us
    all_to_all x1, blocking collectives, shards(): lax.all_to_all(grad_rows.reshape(enc_count, blk_count, CAP, CODE_BREADTH)...  16.4 us
    all_to_all x1, waiting for transfers between devices, shards(): lax.all_to_all(lax.all_to_all(outgoing, 'enc', split_axis=0, concat_axis=...  15.2 us
    all_to_all x1, waiting for transfers between devices, shards(): lax.all_to_all(lax.all_to_all(grad_rows.reshape(enc_count, blk_count, CAP...  12.5 us
    ppermute x2, waiting for transfers between devices, from_behind(): lax.ppermute(value, axis, [(source, source + steps) for source in range(i...  10.2 us
    all_to_all x1, starting transfers between devices, shards(): lax.all_to_all(lax.all_to_all(outgoing, 'enc', split_axis=0, concat_axis=...  8.58 us
  transfers between devices with their start and end apart: 7, of which 7 were waited for; matrix products, arithmetic and copies ran while one was open for 4% of the time, Pallas kernels for 0%

commit v1 on v0

--- a/solution.py
+++ b/solution.py
@@ -1,13 +1,24 @@
+import functools
 import math
 import jax
 import jax.numpy as jnp
 from jax import lax
 from jax.sharding import PartitionSpec as P
+from jax.lax import psum
 
 CODE_BREADTH = 512
 LON = 1440
 MODES = 128
 CAP = 2
+
+
+def answer_arrays(vals, which_axis, net_axis):
+    for i0 in (which_axis, net_axis):
+        vals = psum(vals, i0)
+    return vals
+
+
+_launch_rounds = functools.partial(answer_arrays, which_axis="enc", net_axis="blk")
 
 
 def extended(block, sides, width):
@@ -139,8 +150,8 @@
         observations, pre1, hidden, grad_latent, w_in, w_out
     )
     observed_factor = 1.0 / math.sqrt(devices * slot_total)
-    input_gradient_total, output_gradient_total, blend_matrix_slope_summed = lax.psum(
-        (in_local, out_local, mix_local), ("enc", "blk")
+    input_gradient_total, output_gradient_total, blend_matrix_slope_summed = _launch_rounds(
+        (in_local, out_local, mix_local)
     )
     return (
         predicted_state[None],

time: 428 us -> 386 us (0.902)
  waiting for transfers between devices: 305 us -> 263 us
    psum x1 -> x2, waiting for transfers between devices: 258 us -> 216 us  [answer_arrays(): vals = psum(vals, i0)]
  transfers between devices with their start and end apart: 7 -> 8, of which waited for: 7 -> 8; matrix products, arithmetic and copies ran while one was open for 4% -> 4% of each run, Pallas kernels for 0% -> 0%
where the time goes in v1:
time: 386 us; the launch traced here: 385 us
  waiting for transfers between devices  263 us (68%)
  blocking collectives  33.7 us (9%)
  matrix products  31.5 us (8%)
  starting transfers between devices  22.4 us (6%)
  between operations  14.4 us (4%)
  other arithmetic  11.5 us (3%)
  local copies, waits for them, and re-layouts  8.33 us (2%)
    psum x2, waiting for transfers between devices, answer_arrays(): vals = psum(vals, i0)  216 us
    all_to_all x1, blocking collectives, shards(): lax.all_to_all(outgoing, 'enc', split_axis=0, concat_axis=0, tiled=True)  17.3 us
    all_to_all x1, blocking collectives, shards(): lax.all_to_all(grad_rows.reshape(enc_count, blk_count, CAP, CODE_BREADTH)...  16.4 us
    all_to_all x1, waiting for transfers between devices, shards(): lax.all_to_all(lax.all_to_all(outgoing, 'enc', split_axis=0, concat_axis=...  15.2 us
    all_to_all x1, waiting for transfers between devices, shards(): lax.all_to_all(lax.all_to_all(grad_rows.reshape(enc_count, blk_count, CAP...  12.5 us
    ppermute x2, waiting for transfers between devices, from_behind(): lax.ppermute(value, axis, [(source, source + steps) for source in range(i...  10.2 us
    all_to_all x1, starting transfers between devices, shards(): lax.all_to_all(lax.all_to_all(outgoing, 'enc', split_axis=0, concat_axis=...  8.58 us
  transfers between devices with their start and end apart: 8, of which 8 were waited for; matrix products, arithmetic and copies ran while one was open for 4% of the time, Pallas kernels for 0%

profile of v1, /device:TPU:8, one launch (start us, length us, event | category | flops | bytes accessed | tf_op | source)
XLA Modules:
  0.0 385.0 jit_solution(15690295101010344128)
XLA Ops:
  11.2 17.3 %all_to_all.20 = bf16[16,16,2,512]{3,2,1,0:T(2,128)(2,1)S(1)} all-to-all(bf16[16,16,2,512]{3,2,1,0:T(2,128)(2,1)S(1)} %reshape.48), channel_id=1, replica_groups=mesh['enc'=16,'blk'=16] {'enc'}, dimensions={0} | all-to-all | bytes 1048576 | tf_op jit(solution)/shard_map/all_to_all | solution.py:93
  29.8 8.6 %all-to-all-start.1 = ((bf16[16,16,2,512]{3,2,0,1:T(2,128)(2,1)}), bf16[16,16,2,512]{3,2,0,1:T(2,128)(2,1)S(1)}, u32[]{:S(2)}, u32[]{:S(2)}) async-start(bf16[16,16,2,512]{3,2,0,1:T(2,128)(2,1)} %copy.30), calls=%async_computation.1 | async-start | bytes 1048576 | tf_op jit(solution)/shard_map/all_to_all | solution.py:92
  39.2 15.2 %all-to-all-done.1 = bf16[16,16,2,512]{3,2,0,1:T(2,128)(2,1)S(1)} async-done(((bf16[16,16,2,512]{3,2,0,1:T(2,128)(2,1)}), bf16[16,16,2,512]{3,2,0,1:T(2,128)(2,1)S(1)}, u32[]{:S(2)}, u32[]{:S(2)}) %all-to-all-start.1) | async-done | bytes 524320 | tf_op jit(solution)/shard_map/all_to_all | solution.py:92
  56.1 2.9 collective-permute-start.1
  59.1 2.7 collective-permute-start
  61.8 3.5 fusion.44
  65.3 4.1 %multiply_convert_fusion.2 = (bf16[128,1440]{1,0:T(8,128)(2,1)S(1)}, bf16[128,1440]{1,0:T(8,128)(2,1)}) fusion(f32[128]{0:T(128)S(1)} %fusion.48), kind=kLoop, calls=%fused_computation.45 | loop fusion | flops 2580480 | bytes 737792 | tf_op jit(solution)/shard_map/convert.3
  70.8 5.1 %collective-permute-done.1 = bf16[1,1440,512]{2,1,0:T(8,128)(2,1)S(1)} collective-permute-done((bf16[1,1440,512]{2,1,0:T(8,128)(2,1)S(1)}, bf16[1,1440,512]{2,1,0:T(8,128)(2,1)S(1)}, u32[]{:S(2)}, u32[]{:S(2)}) %collective-permute-start.1) | collective-permute-done | bytes 1474592 | tf_op jit(solution)/shard_map/ppermute | solution.py:32
  77.3 4.6 %collective-permute-done = bf16[1,1440,512]{2,1,0:T(8,128)(2,1)S(1)} collective-permute-done((bf16[1,1440,512]{2,1,0:T(8,128)(2,1)S(1)}, bf16[1,1440,512]{2,1,0:T(8,128)(2,1)S(1)}, u32[]{:S(2)}, u32[]{:S(2)}) %collective-permute-start) | collective-permute-done | bytes 1474592 | tf_op jit(solution)/shard_map/ppermute | solution.py:29
  83.1 2.9 convolution_convert_fusion.1
  85.9 5.2 %fusion = (bf16[1440,512]{1,0:T(8,128)(2,1)S(1)}, bf16[1,1440,512]{2,1,0:T(8,128)(2,1)}) fusion(bf16[1,1440,512]{2,1,0:T(8,128)(2,1)} %param.19, bf16[1440,512]{1,0:T(8,128)(2,1)} %copy-done.12, bf16[1440,512]{1,0:T(8,128)(2,1)S(1)} %convolution_convert_fusion.1, bf16[512,512]{1,0:T(8,128)(2,1)S(1)} %copy-done), kind=kOutput, calls=%fused_computation.4 | convolution fusion | flops 765296640 | bytes 7897088 | tf_op jit(solution)/shard_map/dot_general | solution.py:116
  91.1 4.2 %broadcast_multiply_fusion.3 = (f32[256,512]{1,0:T(8,128)}, f32[256,512]{1,0:T(8,128)}, f32[256,512]{1,0:T(8,128)}) fusion(f32[512]{0:T(512)S(1)} %bitcast.57, f32[512]{0:T(512)S(1)} %bitcast.55, bf16[1440,512]{1,0:T(8,128)(2,1)S(1)} %get-tuple-element.41, bf16[512,512]{1,0:T(8,128)(2,1)S(1)} %copy-done, bf16[128,1440]{1,0:T(8,128)(2,1)} %get-tuple-element.46, ...), kind=kOutput, calls=%fused_computation.57 | convolution fusion | flops 1134936064 | bytes 4313088 | tf_op jit(solution)/shard_map/dot_general | solution.py:126
  95.3 1.9 collective-permute-start.2
  97.2 2.6 collective-permute-start.3
  99.8 4.4 %collective-permute-done.2 = f32[256,512]{1,0:T(8,128)S(1)} collective-permute-done((f32[256,512]{1,0:T(8,128)}, f32[256,512]{1,0:T(8,128)S(1)}, u32[]{:S(2)}, u32[]{:S(2)}) %collective-permute-start.2) | collective-permute-done | bytes 524320 | tf_op jit(solution)/shard_map/ppermute | solution.py:40
  104.2 5.8 %collective-permute-done.3 = f32[256,512]{1,0:T(8,128)S(1)} collective-permute-done((f32[256,512]{1,0:T(8,128)}, f32[256,512]{1,0:T(8,128)S(1)}, u32[]{:S(2)}, u32[]{:S(2)}) %collective-permute-start.3) | collective-permute-done | bytes 524320 | tf_op jit(solution)/shard_map/ppermute | solution.py:40
  110.9 3.9 %fusion.17 = bf16[512,512]{1,0:T(8,128)(2,1)S(1)} fusion(s32[512]{0:T(512)S(1)} %bitcast.60, pred[512]{0:T(512)(128)(4,1)S(1)} %lt.38, bf16[1,1440,512]{2,1,0:T(8,128)(2,1)} %param.19, f32[1440]{0:T(1024)S(1)} %broadcast_maximum_fusion, f32[256,512]{1,0:T(8,128)} %copy-done.16, f32[256,512]{1,0:T(8,128)S(1)} %collective-permute-done.2, ...), kind=kOutput, calls=%fused_computation.24 | convolution fusion | flops 1139146752 | bytes 4841600 | tf_op jit(solution)/shard_map/dot_general | solution.py:134
  115.0 16.4 %all_to_all.21 = bf16[16,16,2,512]{3,2,1,0:T(2,128)(2,1)S(1)} all-to-all(bf16[16,16,2,512]{3,2,1,0:T(2,128)(2,1)S(1)} %reshape.50), channel_id=1, replica_groups=mesh['enc'=16,'blk'=16] {'enc'}, dimensions={0} | all-to-all | bytes 1048576 | tf_op jit(solution)/shard_map/all_to_all | solution.py:136
  132.6 3.6 all-to-all-start.3
  136.2 3.4 fusion.53
  139.6 12.5 %all-to-all-done.3 = bf16[16,16,2,512]{3,2,0,1:T(2,128)(2,1)S(1)} async-done(((bf16[16,16,2,512]{3,2,0,1:T(2,128)(2,1)}), bf16[16,16,2,512]{3,2,0,1:T(2,128)(2,1)S(1)}, u32[]{:S(2)}, u32[]{:S(2)}) %all-to-all-start.3) | async-done | bytes 524320 | tf_op jit(solution)/shard_map/all_to_all | solution.py:135
  152.8 2.0 fusion.20
  157.4 97.7 %all-reduce.7.cloned.1.call-done = (f32[128,512]{0,1:T(8,128)}, f32[512,512]{1,0:T(8,128)}, f32[512,512]{1,0:T(8,128)}) async-done(((f32[128,512]{0,1:T(8,128)}, f32[512,512]{1,0:T(8,128)}, f32[512,512]{1,0:T(8,128)}), (f32[128,512]{0,1:T(8,128)}, f32[512,512]{1,0:T(8,128)}, f32[512,512]{1,0:T(8,128)})) %all-reduce.7.cloned.1.call-update) | async-done | bytes 2359312 | tf_op jit(solution)/shard_map/psum | solution.py:17
  256.1 117.9 %all-reduce.5.cloned.1.call-done = (f32[128,512]{0,1:T(8,128)}, f32[512,512]{1,0:T(8,128)}, f32[512,512]{1,0:T(8,128)}) async-done(((f32[128,512]{0,1:T(8,128)}, f32[512,512]{1,0:T(8,128)}, f32[512,512]{1,0:T(8,128)}), (f32[128,512]{0,1:T(8,128)}, f32[512,512]{1,0:T(8,128)}, f32[512,512]{1,0:T(8,128)})) %all-reduce.5.cloned.1.call-update) | async-done | bytes 2359312 | tf_op jit(solution)/shard_map/psum | solution.py:17
  (69 shorter events, 22.4 us)
Async XLA Ops:
  7.2 78.7 %copy-start = (bf16[512,512]{1,0:T(8,128)(2,1)S(1)}, bf16[512,512]{1,0:T(8,128)(2,1)}, u32[]{:S(2)}) copy-start(bf16[512,512]{1,0:T(8,128)(2,1)} %param.18) | copy-start | bytes 1572868
  11.2 27.2 %copy-start.11 = (s32[1,256]{1,0:T(1,128)S(1)}, s32[1,256]{1,0:T(1,128)}, u32[]{:S(2)}) copy-start(s32[1,256]{1,0:T(1,128)} %param.12) | copy-start | bytes 3076
  11.2 27.5 %copy-start.19 = (s32[1,512]{1,0:T(1,128)S(1)}, s32[1,512]{1,0:T(1,128)}, u32[]{:S(2)}) copy-start(s32[1,512]{1,0:T(1,128)} %param.11) | copy-start | bytes 6148
  29.8 24.6 %all-to-all-start.1 = ((bf16[16,16,2,512]{3,2,0,1:T(2,128)(2,1)}), bf16[16,16,2,512]{3,2,0,1:T(2,128)(2,1)S(1)}, u32[]{:S(2)}, u32[]{:S(2)}) async-start(bf16[16,16,2,512]{3,2,0,1:T(2,128)(2,1)} %copy.30), calls=%async_computation.1 | async-start | bytes 1048576 | tf_op jit(solution)/shard_map/all_to_all | solution.py:92
  56.1 14.7 %copy-start.12 = (bf16[1440,512]{1,0:T(8,128)(2,1)}, bf16[1440,512]{1,0:T(8,128)(2,1)S(1)}, u32[]{:S(2)}) copy-start(bf16[1440,512]{1,0:T(8,128)(2,1)S(1)} %divide_convert_fusion.1) | copy-start | bytes 4423684
  56.1 13.3 %copy-start.14 = (f32[256,512]{1,0:T(8,128)S(1)}, f32[256,512]{1,0:T(8,128)}, u32[]{:S(2)}) copy-start(f32[256,512]{1,0:T(8,128)} %param.15) | copy-start | bytes 1572868
  56.1 19.8 %collective-permute-start.1 = (bf16[1,1440,512]{2,1,0:T(8,128)(2,1)S(1)}, bf16[1,1440,512]{2,1,0:T(8,128)(2,1)S(1)}, u32[]{:S(2)}, u32[]{:S(2)}) collective-permute-start(bf16[1,1440,512]{2,1,0:T(8,128)(2,1)S(1)} %bitcast.52), channel_id=1, source_target_pairs={{1,0},{2,1},{3,2},{4,3},{5,4},{6,5},{7,6},{8,7},{9,8},{10,9},{11,1... | collective-permute-start | bytes 4423688 | tf_op jit(solution)/shard_map/ppermute | solution.py:32
  59.1 22.8 %collective-permute-start = (bf16[1,1440,512]{2,1,0:T(8,128)(2,1)S(1)}, bf16[1,1440,512]{2,1,0:T(8,128)(2,1)S(1)}, u32[]{:S(2)}, u32[]{:S(2)}) collective-permute-start(bf16[1,1440,512]{2,1,0:T(8,128)(2,1)S(1)} %bitcast.53), channel_id=1, source_target_pairs={{0,1},{1,2},{2,3},{3,4},{4,5},{5,6},{6,7},{7,8},{8,9},{9,10},{10,1... | collective-permute-start | bytes 4423688 | tf_op jit(solution)/shard_map/ppermute | solution.py:29
  65.3 17.7 %copy-start.8 = (bf16[128,1440]{1,0:T(8,128)(2,1)}, bf16[128,1440]{1,0:T(8,128)(2,1)S(1)}, u32[]{:S(2)}) copy-start(bf16[128,1440]{1,0:T(8,128)(2,1)S(1)} %get-tuple-element.48) | copy-start | bytes 1105924
  65.3 17.7 %copy-start.9 = (bf16[128,1440]{1,0:T(8,128)(2,1)}, bf16[128,1440]{1,0:T(8,128)(2,1)S(1)}, u32[]{:S(2)}) copy-start(bf16[128,1440]{1,0:T(8,128)(2,1)S(1)} %get-tuple-element.49) | copy-start | bytes 1105924
  69.4 13.6 %copy-start.10 = (bf16[128,1440]{1,0:T(8,128)(2,1)}, bf16[128,1440]{1,0:T(8,128)(2,1)S(1)}, u32[]{:S(2)}) copy-start(bf16[128,1440]{1,0:T(8,128)(2,1)S(1)} %get-tuple-element.45) | copy-start | bytes 1105924
  69.4 6.5 %copy-start.17 = (f32[1,512]{1,0:T(1,128)S(1)}, f32[1,512]{1,0:T(1,128)}, u32[]{:S(2)}) copy-start(f32[1,512]{1,0:T(1,128)} %param.17) | copy-start | bytes 6148
  76.0 7.1 %copy-start.18 = (f32[1,512]{1,0:T(1,128)S(1)}, f32[1,512]{1,0:T(1,128)}, u32[]{:S(2)}) copy-start(f32[1,512]{1,0:T(1,128)} %param.16) | copy-start | bytes 6148
  91.1 4.2 %copy-start.1 = (bf16[1440,512]{1,0:T(8,128)(2,1)}, bf16[1440,512]{1,0:T(8,128)(2,1)S(1)}, u32[]{:S(2)}) copy-start(bf16[1440,512]{1,0:T(8,128)(2,1)S(1)} %get-tuple-element.41) | copy-start | bytes 4423684
  95.3 8.9 %collective-permute-start.2 = (f32[256,512]{1,0:T(8,128)}, f32[256,512]{1,0:T(8,128)S(1)}, u32[]{:S(2)}, u32[]{:S(2)}) collective-permute-start(f32[256,512]{1,0:T(8,128)} %get-tuple-element.43), channel_id=1, source_target_pairs={{1,0},{2,1},{3,2},{4,3},{5,4},{6,5},{7,6},{8,7},{9,8},{10,9},{11,1... | collective-permute-start | bytes 1572872 | tf_op jit(solution)/shard_map/ppermute | solution.py:40
  97.2 12.8 %collective-permute-start.3 = (f32[256,512]{1,0:T(8,128)}, f32[256,512]{1,0:T(8,128)S(1)}, u32[]{:S(2)}, u32[]{:S(2)}) collective-permute-start(f32[256,512]{1,0:T(8,128)} %get-tuple-element.44), channel_id=1, source_target_pairs={{0,1},{1,2},{2,3},{3,4},{4,5},{5,6},{6,7},{7,8},{8,9},{9,10},{10,1... | collective-permute-start | bytes 1572872 | tf_op jit(solution)/shard_map/ppermute | solution.py:40
  132.6 19.5 %all-to-all-start.3 = ((bf16[16,16,2,512]{3,2,0,1:T(2,128)(2,1)}), bf16[16,16,2,512]{3,2,0,1:T(2,128)(2,1)S(1)}, u32[]{:S(2)}, u32[]{:S(2)}) async-start(bf16[16,16,2,512]{3,2,0,1:T(2,128)(2,1)} %copy.32), calls=%async_computation.3 | async-start | bytes 1048576 | tf_op jit(solution)/shard_map/all_to_all | solution.py:135
  136.2 118.9 %all-reduce.7.cloned.1.call-start = ((), (), s32[]{:S(2)}) async-start(), calls=%async_computation.5 | async-start | bytes 4718592 | tf_op jit(solution)/shard_map/psum | solution.py:17
  139.6 13.2 %copy-start.15 = (bf16[512,512]{1,0:T(8,128)(2,1)S(1)}, bf16[512,512]{1,0:T(8,128)(2,1)}, u32[]{:S(2)}) copy-start(bf16[512,512]{1,0:T(8,128)(2,1)} %param.14) | copy-start | bytes 1572868
  152.8 2.0 copy-start.3
  157.4 97.8 %copy-start.7 = (bf16[128,512]{1,0:T(8,128)(2,1)S(1)}, bf16[128,512]{1,0:T(8,128)(2,1)}, u32[]{:S(2)}) copy-start(bf16[128,512]{1,0:T(8,128)(2,1)} %param.13) | copy-start | bytes 393220
  157.4 216.6 %all-reduce.5.cloned.1.call-start = ((), (), s32[]{:S(2)}) async-start(), calls=%async_computation.4 | async-start | bytes 4718592 | tf_op jit(solution)/shard_map/psum | solution.py:17
  374.0 2.0 copy-start.5
  374.0 3.1 copy-start.4
  (4 other events, 4.4 us)
Sparse Core Ops, SparseCore 0:
  157.5 97.6 all-reduce.6
  257.9 116.0 all-reduce.4
